TPU v7x, 128 devices: a whole 4x4x4 slice. The times are simulated.
128 devices in a mesh: grid: 64 (over x, y, z_lo, core), col: 2 (over z_hi).
Axes of the slice: x: 4, y: 4, z: 4 (z_hi: 2, z_lo: 2; z = z_hi * 2 + z_lo), core: 2. Of those that a mesh axis runs over, the one named last changes fastest.
Arguments:
- orbitals: bfloat16 [884736, 256], P(('grid', 'col')), may hold values from -6 to 6
- points: int32 [1024], replicated, may hold values from 0 to 884735, as said below
- cinv: bfloat16 [1024, 256], replicated, may hold values from -0.1875 to 0.1875
Outputs:
- potential: bfloat16 [256, 884736], P(None, ('grid', 'col'))
- coupling: float32 [1024, 256], P(('grid', 'col'))
Inputs may be any that keep to these rules, and one draw needn't show every extreme that they name: `points`: 1024 distinct grid rows.
All inputs are finite; a program needn't handle non-finite values.
Results may differ from a plain program's by a relative error of at most 0.0046.
Values may be sent and summed in bfloat16 or wider, within the bound.
A program may use at most 192 MiB of HBM per device.

v0:
```python
import math
import jax
import jax.numpy as jnp
from jax import lax
from jax.sharding import PartitionSpec as P

NX = 96
screening = 0.25


def kernel_table(size):
    index = jnp.arange(size)
    wave = jnp.where(index < (size + 1) // 2, index, index - size).astype(jnp.float32) * (
        2.0 * math.pi / size
    )
    squared = wave[:, None, None] ** 2 + wave[None, :, None] ** 2 + wave[None, None, :] ** 2
    return jnp.where(squared > 0, 1.0 / (squared + screening), 0.0)


def along(table, values, axis):
    forms = {1: "kn,cnyz->ckyz", 2: "kn,cxnz->cxkz", 3: "kn,cxyn->cxyk"}
    return jnp.einsum(forms[axis], table, values, precision=lax.Precision.HIGHEST)


def screened_solve(field):
    size = field.shape[1]
    index = jnp.arange(size, dtype=jnp.int32)
    phase = index[:, None] * index[None, :] % size
    angle = phase.astype(jnp.float32) * (2.0 * math.pi / size)
    cos_table = jnp.cos(angle)
    sin_table = jnp.sin(angle)
    real_part = along(cos_table, field, 3)
    imag_part = -along(sin_table, field, 3)
    for axis in (2, 1):
        real_part, imag_part = (
            along(cos_table, real_part, axis) + along(sin_table, imag_part, axis),
            along(cos_table, imag_part, axis) - along(sin_table, real_part, axis),
        )
    weights = kernel_table(size)
    real_part = real_part * weights
    imag_part = imag_part * weights
    for axis in (1, 2):
        real_part, imag_part = (
            along(cos_table, real_part, axis) - along(sin_table, imag_part, axis),
            along(cos_table, imag_part, axis) + along(sin_table, real_part, axis),
        )
    result = along(cos_table, real_part, 3) - along(sin_table, imag_part, 3)
    return result / float(size**3)


def local(orbitals, points, cinv):
    ranks = lax.axis_size(("grid", "col"))
    local_rows = orbitals.shape[0]
    orbital_count = orbitals.shape[1]
    npoints = cinv.shape[0]
    columns = cinv.shape[1]
    per_rank = columns // ranks
    first_row = lax.axis_index(("grid", "col")) * local_rows
    offset = points - first_row
    inside = (offset >= 0) & (offset < local_rows)
    picked = jnp.take(orbitals, jnp.clip(offset, 0, local_rows - 1), axis=0)
    picked = jnp.where(inside[:, None], picked.astype(jnp.float32), 0.0)
    point_rows = lax.psum(picked, ("grid", "col")).astype(jnp.bfloat16)
    scale = 1.0 / math.sqrt(orbital_count)
    block_rows = math.gcd(local_rows, 1152)

    def pair_block(block):
        product = (
            lax.dot_general(
                block, point_rows, (((1,), (1,)), ((), ())), preferred_element_type=jnp.float32
            )
            * scale
        )
        return (product * product).astype(jnp.bfloat16)

    pairs = lax.map(
        pair_block, orbitals.reshape(local_rows // block_rows, block_rows, orbital_count)
    )
    pairs = pairs.reshape(local_rows, npoints)
    theta_cols = lax.dot_general(
        cinv, pairs, (((0,), (1,)), ((), ())), preferred_element_type=jnp.float32
    )
    fields = lax.all_to_all(theta_cols, ("grid", "col"), split_axis=0, concat_axis=1, tiled=True)
    fields = fields.reshape(per_rank, NX, NX, NX)
    potentials = screened_solve(fields).astype(jnp.bfloat16).reshape(per_rank, NX * NX * NX)
    rows_back = lax.all_to_all(potentials, ("grid", "col"), split_axis=1, concat_axis=0, tiled=True)
    factor = math.sqrt(npoints) / float(NX**3)
    coupling = lax.psum_scatter(
        lax.dot_general(
            pairs, rows_back, (((0,), (1,)), ((), ())), preferred_element_type=jnp.float32
        )
        * factor,
        ("grid", "col"),
        scatter_dimension=0,
        tiled=True,
    )
    return (rows_back, coupling)


def solution(mesh):
    in_specs = (P(("grid", "col"), None), P(), P())
    out_specs = (P(None, ("grid", "col")), P(("grid", "col"), None))
    return jax.shard_map(local, mesh=mesh, in_specs=in_specs, out_specs=out_specs, check_vma=False)
```

profile of v0, /device:TPU:0, one launch (start us, length us, event | category | flops | bytes accessed | tf_op | source)
XLA Modules:
  0.0 1324.5 jit_solution(9655108853187020111)
XLA Ops:
  7.2 0.8 compare_and_fusion.1
  7.9 0.7 fusion.144
  8.6 5.9 gather_fusion
  14.9 74.1 %all-reduce.1 = bf16[1024,256]{1,0:T(8,128)(2,1)S(1)} all-reduce(f32[1024,256]{1,0:T(8,128)S(1)} %convert_select_fusion), channel_id=1, replica_groups=mesh['grid'=64,'col'=2] {'grid','col'}, use_global_device_ids=true, to_apply=%region_0.1 | all-reduce | flops 262144 | bytes 1572864 | tf_op jit(solution)/shard_map/psum | solution.py:63
  89.0 19.9 %while.10 = (s32[]{:T(128)}, bf16[6,1152,1024]{2,1,0:T(8,128)(2,1)}, bf16[6,1152,256]{2,1,0:T(8,128)(2,1)}, bf16[1024,256]{1,0:T(8,128)(2,1)S(1)}, s32[]{:T(128)}) while((s32[]{:T(128)}, bf16[6,1152,1024]{2,1,0:T(8,128)(2,1)}, bf16[6,1152,256]{2,1,0:T(8,128)(2,1)}, bf16[1024,256]{1,0:T(8,128)(2,1)S(1)}, s32[]{:T(128)}) %tuple.28), condition=%wide.region_2.3_spmd, body=%wide.region_1.2_spmd.sunk | while | flops 607518720 | bytes 3474501 | solution.py:76
  89.0 3.3 fusion.234
  92.3 3.3 fusion.234
  95.7 3.3 fusion.234
  99.0 3.4 fusion.234
  102.3 3.3 fusion.234
  105.6 3.3 fusion.234
  109.0 11.7 convolution_bitcast_fusion
  120.7 9.1 all_to_all.26
  129.8 6.9 all-to-all-start
  137.1 3.1 fusion.18
  140.1 81.1 %all-to-all-done = f32[128,2,6912]{2,1,0:T(2,128)} async-done(((f32[128,2,6912]{2,1,0:T(2,128)}), f32[128,2,6912]{2,1,0:T(2,128)}, u32[]{:S(2)}, u32[]{:S(2)}) %all-to-all-start) | async-done | bytes 7077920 | tf_op jit(solution)/shard_map/all_to_all | solution.py:83
  221.2 6.4 copy.15
  227.6 10.6 reshape.103
  238.2 11.3 fusion.39
  249.5 21.2 %fusion.57 = f32[2,96,96,96]{2,3,1,0:T(8,128)S(1)} fusion(f32[2,96,96,96]{3,2,1,0:T(8,128)S(1)} %copy-done.6), kind=kOutput, calls=%fused_computation.66 | convolution fusion | flops 2038514688 | bytes 14155776 | tf_op jit(solution)/shard_map/kn,cxyn->cxyk/dot_general | solution.py:22
  270.7 8.8 fusion.55
  279.5 10.5 fusion.36
  290.0 19.2 %subtract_bitcast_fusion.1 = f32[2,96,96,96]{2,3,1,0:T(8,128)} fusion(f32[2,96,96,96]{3,2,1,0:T(8,128)} %fusion.36, f32[2,96,96,96]{3,2,1,0:T(8,128)S(1)} %fusion.39), kind=kOutput, calls=%fused_computation.21 | convolution fusion | flops 2042053632 | bytes 21233664 | tf_op jit(solution)/shard_map/kn,cxnz->cxkz/dot_general | solution.py:22
  309.2 17.8 %add_bitcast_fusion.1 = f32[2,96,96,96]{2,3,1,0:T(8,128)} fusion(f32[2,96,96,96]{3,2,1,0:T(8,128)S(1)} %fusion.55, f32[2,96,96,96]{3,2,1,0:T(8,128)S(1)} %fusion.39), kind=kOutput, calls=%fused_computation.22 | convolution fusion | flops 2042053632 | bytes 21233664 | tf_op jit(solution)/shard_map/kn,cxnz->cxkz/dot_general | solution.py:22
  326.9 12.4 copy.18
  339.3 12.4 copy.21
  351.7 13.4 %fusion.48 = f32[2,96,96,96]{3,2,1,0:T(8,128)} fusion(f32[2,96,96,96]{1,3,2,0:T(8,128)} %copy.21), kind=kOutput, calls=%fused_computation.57 | convolution fusion | flops 2038514688 | bytes 14155776 | tf_op jit(solution)/shard_map/kn,cnyz->ckyz/dot_general | solution.py:22
  365.1 10.2 fusion.53
  375.3 11.3 bitcast_multiply_fusion
  386.6 15.4 %bitcast_multiply_fusion.1 = f32[2,96,96,96]{1,3,2,0:T(8,128)S(1)} fusion(f32[2,96,96,96]{3,2,1,0:T(8,128)} %fusion.53, f32[96,96,96]{0,2,1:T(8,128)S(1)} %bitcast.109, f32[2,96,96,96]{1,3,2,0:T(8,128)} %copy.21), kind=kOutput, calls=%fused_computation.15 | convolution fusion | flops 2042053632 | bytes 24772608 | tf_op jit(solution)/shard_map/kn,cnyz->ckyz/dot_general | solution.py:22
  402.0 10.3 fusion.50
  412.3 8.8 fusion.44
  421.1 10.6 add_bitcast_fusion
  431.7 12.4 copy.31
  444.1 26.4 %fusion.41 = f32[2,96,96,96]{2,3,1,0:T(8,128)} fusion(f32[2,96,96,96]{2,3,1,0:T(8,128)} %copy.31), kind=kOutput, calls=%fused_computation.50 | convolution fusion | flops 2038514688 | bytes 14155776 | tf_op jit(solution)/shard_map/kn,cxnz->cxkz/dot_general | solution.py:22
  470.6 23.6 %fusion.30 = f32[2,96,96,96]{2,3,1,0:T(8,128)} fusion(f32[2,96,96,96]{2,3,1,0:T(8,128)S(1)} %copy-done.3), kind=kOutput, calls=%fused_computation.39 | convolution fusion | flops 2038514688 | bytes 14155776 | tf_op jit(solution)/shard_map/kn,cxnz->cxkz/dot_general | solution.py:22
  494.3 10.6 subtract_bitcast_fusion
  504.8 12.5 copy.30
  517.4 24.6 %fusion.28 = f32[2,96,96,96]{2,3,1,0:T(8,128)S(1)} fusion(f32[2,96,96,96]{2,3,1,0:T(8,128)} %copy.30), kind=kOutput, calls=%fused_computation.37 | convolution fusion | flops 2038514688 | bytes 14155776 | tf_op jit(solution)/shard_map/kn,cxnz->cxkz/dot_general | solution.py:22
  542.0 23.4 %fusion.46 = f32[2,96,96,96]{2,3,1,0:T(8,128)} fusion(f32[2,96,96,96]{2,3,1,0:T(8,128)S(1)} %copy-done.4), kind=kOutput, calls=%fused_computation.55 | convolution fusion | flops 2038514688 | bytes 14155776 | tf_op jit(solution)/shard_map/kn,cxnz->cxkz/dot_general | solution.py:22
  565.4 10.2 fusion.7
  575.6 15.9 %multiply_convert_fusion = bf16[2,96,96,96]{3,2,1,0:T(8,128)(2,1)} fusion(f32[2,96,96,96]{3,2,1,0:T(8,128)} %fusion.7, f32[2,96,96,96]{2,3,1,0:T(8,128)} %fusion.46, f32[2,96,96,96]{2,3,1,0:T(8,128)} %fusion.30), kind=kOutput, calls=%fused_computation.16 | convolution fusion | flops 2045592576 | bytes 24772608 | tf_op jit(solution)/shard_map/kn,cxyn->cxyk/dot_general | solution.py:22
  591.5 7.8 all_to_all.29
  599.3 5.6 copy.24
  604.9 55.8 %all_to_all.35 = bf16[2,128,6912]{2,0,1:T(2,128)(2,1)} all-to-all(bf16[2,128,6912]{2,0,1:T(2,128)(2,1)S(1)} %copy.24), channel_id=1, replica_groups=mesh['grid'=64,'col'=2] {'grid','col'}, dimensions={1} | all-to-all | bytes 7077888 | tf_op jit(solution)/shard_map/all_to_all | solution.py:86
  660.7 8.3 all_to_all.32
  669.0 10.9 convolution_multiply_fusion.1
  679.9 637.2 %reduce-scatter.2.cloned.1.call-done = f32[8,256]{1,0:T(8,128)} async-done(((f32[1024,256]{1,0:T(8,128)}), f32[8,256]{1,0:T(8,128)}) %reduce-scatter.2.cloned.1.call-update) | async-done | bytes 8208 | tf_op jit(solution)/shard_map/reduce_scatter | solution.py:88
  (46 shorter events, 0.8 us)
Async XLA Ops:
  7.2 101.8 %copy-start = (bf16[1024,256]{1,0:T(8,128)(2,1)S(1)}, bf16[1024,256]{1,0:T(8,128)(2,1)}, u32[]{:S(2)}) copy-start(bf16[1024,256]{1,0:T(8,128)(2,1)} %param.7) | copy-start | bytes 1572868
  129.8 91.4 %all-to-all-start = ((f32[128,2,6912]{2,1,0:T(2,128)}), f32[128,2,6912]{2,1,0:T(2,128)}, u32[]{:S(2)}, u32[]{:S(2)}) async-start(f32[128,2,6912]{2,1,0:T(2,128)} %all_to_all.26), calls=%async_computation | async-start | bytes 14155776 | tf_op jit(solution)/shard_map/all_to_all | solution.py:83
  136.7 1180.5 %reduce-scatter.2.cloned.1.call-start = ((), (), s32[]{:S(2)}) async-start(), calls=%async_computation.3 | async-start | bytes 1056768 | tf_op jit(solution)/shard_map/reduce_scatter | solution.py:88
  238.2 11.3 copy-start.6
  351.7 13.4 %copy-start.5 = (f32[2,96,96,96]{1,3,2,0:T(8,128)S(1)}, f32[2,96,96,96]{1,3,2,0:T(8,128)}, u32[]{:S(2)}) copy-start(f32[2,96,96,96]{1,3,2,0:T(8,128)} %copy.18) | copy-start | bytes 21233668
  351.7 23.6 %slice-start = ((s8[4718592]{0:T(1024)(128)(4,1)}), s8[4194304]{0:T(1024)(128)(4,1)S(1)}, s32[]{:S(2)}) async-start(s8[4718592]{0:T(1024)(128)(4,1)} %bitcast.108), calls=%async_computation.4 | async-start | bytes 8388608
  365.1 10.2 slice-start.1
  386.6 25.7 %copy-start.2 = (f32[2,96,96,96]{1,3,2,0:T(8,128)}, f32[2,96,96,96]{1,3,2,0:T(8,128)S(1)}, u32[]{:S(2)}) copy-start(f32[2,96,96,96]{1,3,2,0:T(8,128)S(1)} %bitcast_multiply_fusion) | copy-start | bytes 21233668
  444.1 26.4 %copy-start.3 = (f32[2,96,96,96]{2,3,1,0:T(8,128)S(1)}, f32[2,96,96,96]{2,3,1,0:T(8,128)}, u32[]{:S(2)}) copy-start(f32[2,96,96,96]{2,3,1,0:T(8,128)} %copy.31) | copy-start | bytes 21233668
  444.1 50.1 %slice-start.2 = ((s8[9437184]{0:T(1024)(128)(4,1)}), s8[4194304]{0:T(1024)(128)(4,1)S(1)}, s32[]{:S(2)}) async-start(s8[9437184]{0:T(1024)(128)(4,1)} %bitcast.110), calls=%async_computation.6 | async-start | bytes 8388608
  444.1 50.1 %slice-start.3 = ((s8[9437184]{0:T(1024)(128)(4,1)}), s8[4194304]{0:T(1024)(128)(4,1)S(1)}, s32[]{:S(2)}) async-start(s8[9437184]{0:T(1024)(128)(4,1)} %bitcast.110), calls=%async_computation.7 | async-start | bytes 8388608
  444.1 50.1 %slice-start.5 = ((s8[9437184]{0:T(1024)(128)(4,1)}), s8[4194304]{0:T(1024)(128)(4,1)S(1)}, s32[]{:S(2)}) async-start(s8[9437184]{0:T(1024)(128)(4,1)} %bitcast.112), calls=%async_computation.9 | async-start | bytes 8388608
  444.1 50.1 %slice-start.6 = ((s8[9437184]{0:T(1024)(128)(4,1)}), s8[4194304]{0:T(1024)(128)(4,1)S(1)}, s32[]{:S(2)}) async-start(s8[9437184]{0:T(1024)(128)(4,1)} %bitcast.112), calls=%async_computation.10 | async-start | bytes 8388608
  470.6 23.7 %slice-start.4 = ((s8[9437184]{0:T(1024)(128)(4,1)}), s8[1048576]{0:T(1024)(128)(4,1)S(1)}, s32[]{:S(2)}) async-start(s8[9437184]{0:T(1024)(128)(4,1)} %bitcast.110), calls=%async_computation.8 | async-start | bytes 2097152
  470.6 23.7 %slice-start.7 = ((s8[9437184]{0:T(1024)(128)(4,1)}), s8[1048576]{0:T(1024)(128)(4,1)S(1)}, s32[]{:S(2)}) async-start(s8[9437184]{0:T(1024)(128)(4,1)} %bitcast.112), calls=%async_computation.11 | async-start | bytes 2097152
  517.4 24.6 %copy-start.4 = (f32[2,96,96,96]{2,3,1,0:T(8,128)S(1)}, f32[2,96,96,96]{2,3,1,0:T(8,128)}, u32[]{:S(2)}) copy-start(f32[2,96,96,96]{2,3,1,0:T(8,128)} %copy.30) | copy-start | bytes 21233668
  517.4 48.0 %slice-start.8 = ((s8[9437184]{0:T(1024)(128)(4,1)}), s8[4194304]{0:T(1024)(128)(4,1)S(1)}, s32[]{:S(2)}) async-start(s8[9437184]{0:T(1024)(128)(4,1)} %bitcast.114), calls=%async_computation.12 | async-start | bytes 8388608
  517.4 48.0 %slice-start.9 = ((s8[9437184]{0:T(1024)(128)(4,1)}), s8[4194304]{0:T(1024)(128)(4,1)S(1)}, s32[]{:S(2)}) async-start(s8[9437184]{0:T(1024)(128)(4,1)} %bitcast.114), calls=%async_computation.13 | async-start | bytes 8388608
  542.0 23.4 %slice-start.10 = ((s8[9437184]{0:T(1024)(128)(4,1)}), s8[1048576]{0:T(1024)(128)(4,1)S(1)}, s32[]{:S(2)}) async-start(s8[9437184]{0:T(1024)(128)(4,1)} %bitcast.114), calls=%async_computation.14 | async-start | bytes 2097152
  660.7 656.4 %copy-start.1 = (bf16[1024,256]{1,0:T(8,128)(2,1)S(1)}, bf16[1024,256]{1,0:T(8,128)(2,1)}, u32[]{:S(2)}) copy-start(bf16[1024,256]{1,0:T(8,128)(2,1)} %param.7) | copy-start | bytes 1572868
Sparse Core Ops, SparseCore 0:
  680.1 637.0 reduce-scatter.1
where the time goes:
time: 1330 us; the launch traced here: 1320 us
  waiting for transfers between devices  718 us (54%)
  matrix products  346 us (26%)
  blocking collectives  130 us (10%)
  local copies, waits for them, and re-layouts  103 us (8%)
  between operations  14.8 us (1%)
    reduce_scatter x1, waiting for transfers between devices, local(): lax.psum_scatter(lax.dot_general(pairs, rows_back, (((0,), (1,)), ((), ()...  637 us
    dot_general x20, matrix products, along(): jnp.einsum(forms[axis], table, values, precision=lax.Precision.HIGHEST)  303 us
    all_to_all x1, waiting for transfers between devices, local(): lax.all_to_all(theta_cols, ('grid', 'col'), split_axis=0, concat_axis=1,...  81.1 us
    psum x1, blocking collectives, local(): point_rows = lax.psum(picked, ('grid', 'col')).astype(jnp.bfloat16)  74.1 us
    all_to_all x1, blocking collectives, local(): lax.all_to_all(potentials, ('grid', 'col'), split_axis=1, concat_axis=0,...  55.8 us
  transfers between devices with their start and end apart: 2, of which 2 were waited for; matrix products, arithmetic and copies ran while one was open for 0% of the time, Pallas kernels for 0%

commit v1 on v0

--- a/solution.py
+++ b/solution.py
@@ -3,6 +3,7 @@
 import jax.numpy as jnp
 from jax import lax
 from jax.sharding import PartitionSpec as P
+from jax.lax import psum
 
 NX = 96
 screening = 0.25
@@ -60,7 +61,15 @@
     inside = (offset >= 0) & (offset < local_rows)
     picked = jnp.take(orbitals, jnp.clip(offset, 0, local_rows - 1), axis=0)
     picked = jnp.where(inside[:, None], picked.astype(jnp.float32), 0.0)
-    point_rows = lax.psum(picked, ("grid", "col")).astype(jnp.bfloat16)
+
+    def ticks_tell(vec):
+        axis_id = "grid"
+        dev_axis = "col"
+        for idx in (dev_axis, axis_id):
+            vec = psum(vec, axis_name=idx)
+        return vec
+
+    point_rows = ticks_tell(picked).astype(jnp.bfloat16)
     scale = 1.0 / math.sqrt(orbital_count)
     block_rows = math.gcd(local_rows, 1152)
 

time: 1330 us -> 1600 us (1.20)
  blocking collectives: 130 us -> 344 us
  waiting for transfers between devices: 718 us -> 769 us
    psum x1, blocking collectives: 74.1 us -> 289 us  [ticks_tell(): vec = psum(vec, axis_name=idx)]
    psum x0 -> x1, waiting for transfers between devices: none -> 50.8 us  [ticks_tell(): vec = psum(vec, axis_name=idx)]
  transfers between devices with their start and end apart: 2 -> 3, of which waited for: 2 -> 3; matrix products, arithmetic and copies ran while one was open for 0% -> 0% of each run, Pallas kernels for 0% -> 0%
where the time goes in v1:
time: 1600 us; the launch traced here: 1590 us
  waiting for transfers between devices  769 us (48%)
  matrix products  346 us (22%)
  blocking collectives  344 us (22%)
  local copies, waits for them, and re-layouts  103 us (6%)
    reduce_scatter x1, waiting for transfers between devices, local(): lax.psum_scatter(lax.dot_general(pairs, rows_back, (((0,), (1,)), ((), ()...  637 us
    dot_general x20, matrix products, along(): jnp.einsum(forms[axis], table, values, precision=lax.Precision.HIGHEST)  303 us
    psum x1, blocking collectives, ticks_tell(): vec = psum(vec, axis_name=idx)  289 us
    all_to_all x1, waiting for transfers between devices, local(): lax.all_to_all(theta_cols, ('grid', 'col'), split_axis=0, concat_axis=1,...  81 us
    all_to_all x1, blocking collectives, local(): lax.all_to_all(potentials, ('grid', 'col'), split_axis=1, concat_axis=0,...  55.9 us
    psum x1, waiting for transfers between devices, ticks_tell(): vec = psum(vec, axis_name=idx)  50.8 us
  transfers between devices with their start and end apart: 3, of which 3 were waited for; matrix products, arithmetic and copies ran while one was open for 0% of the time, Pallas kernels for 0%

profile of v1, /device:TPU:0, one launch (start us, length us, event | category | flops | bytes accessed | tf_op | source)
XLA Modules:
  0.0 1589.7 jit_solution(13767758844243913573)
XLA Ops:
  8.7 5.9 gather_fusion
  14.6 1.3 convert_select_fusion
  15.9 50.8 %all-reduce.3.cloned.1.call-done = f32[1024,256]{1,0:T(8,128)} async-done(((f32[1024,256]{1,0:T(8,128)}), f32[1024,256]{1,0:T(8,128)}) %all-reduce.3.cloned.1.call-update) | async-done | bytes 1048592 | tf_op jit(solution)/shard_map/psum | solution.py:69
  66.8 288.5 %all-reduce.4 = bf16[1024,256]{1,0:T(8,128)(2,1)S(1)} all-reduce(f32[1024,256]{1,0:T(8,128)} %all-reduce.3.cloned.1.call-done), channel_id=1, replica_groups=mesh['grid'=64,'col'=2] {'grid'}, use_global_device_ids=true, to_apply=%region_1.2 | all-reduce | flops 262144 | bytes 1572864 | tf_op jit(solution)/shard_map/psum | solution.py:69
  355.3 19.9 %while.10 = (s32[]{:T(128)}, bf16[6,1152,1024]{2,1,0:T(8,128)(2,1)}, bf16[6,1152,256]{2,1,0:T(8,128)(2,1)}, bf16[1024,256]{1,0:T(8,128)(2,1)S(1)}, s32[]{:T(128)}) while((s32[]{:T(128)}, bf16[6,1152,1024]{2,1,0:T(8,128)(2,1)}, bf16[6,1152,256]{2,1,0:T(8,128)(2,1)}, bf16[1024,256]{1,0:T(8,128)(2,1)S(1)}, s32[]{:T(128)}) %tuple.30), condition=%wide.region_3.4_spmd, body=%wide.region_2.3_spmd.sunk | while | flops 607518720 | bytes 3474501 | solution.py:85
  355.3 3.3 fusion.234
  358.6 3.3 fusion.234
  362.0 3.3 fusion.234
  365.3 3.4 fusion.234
  368.6 3.3 fusion.234
  371.9 3.3 fusion.234
  375.3 11.7 convolution_bitcast_fusion
  387.0 9.1 all_to_all.26
  396.1 5.8 all-to-all-start
  402.3 3.1 fusion.18
  405.3 81.0 %all-to-all-done = f32[128,2,6912]{2,1,0:T(2,128)} async-done(((f32[128,2,6912]{2,1,0:T(2,128)}), f32[128,2,6912]{2,1,0:T(2,128)}, u32[]{:S(2)}, u32[]{:S(2)}) %all-to-all-start) | async-done | bytes 7077920 | tf_op jit(solution)/shard_map/all_to_all | solution.py:92
  486.3 6.4 copy.15
  492.7 10.6 reshape.103
  503.3 11.3 fusion.39
  514.6 21.2 %fusion.57 = f32[2,96,96,96]{2,3,1,0:T(8,128)S(1)} fusion(f32[2,96,96,96]{3,2,1,0:T(8,128)S(1)} %copy-done.6), kind=kOutput, calls=%fused_computation.66 | convolution fusion | flops 2038514688 | bytes 14155776 | tf_op jit(solution)/shard_map/kn,cxyn->cxyk/dot_general | solution.py:23
  535.8 8.8 fusion.55
  544.6 10.5 fusion.36
  555.1 19.2 %subtract_bitcast_fusion.1 = f32[2,96,96,96]{2,3,1,0:T(8,128)} fusion(f32[2,96,96,96]{3,2,1,0:T(8,128)} %fusion.36, f32[2,96,96,96]{3,2,1,0:T(8,128)S(1)} %fusion.39), kind=kOutput, calls=%fused_computation.21 | convolution fusion | flops 2042053632 | bytes 21233664 | tf_op jit(solution)/shard_map/kn,cxnz->cxkz/dot_general | solution.py:23
  574.3 17.8 %add_bitcast_fusion.1 = f32[2,96,96,96]{2,3,1,0:T(8,128)} fusion(f32[2,96,96,96]{3,2,1,0:T(8,128)S(1)} %fusion.55, f32[2,96,96,96]{3,2,1,0:T(8,128)S(1)} %fusion.39), kind=kOutput, calls=%fused_computation.22 | convolution fusion | flops 2042053632 | bytes 21233664 | tf_op jit(solution)/shard_map/kn,cxnz->cxkz/dot_general | solution.py:23
  592.0 12.4 copy.18
  604.4 12.4 copy.21
  616.8 13.4 fusion.48
  630.2 10.2 fusion.53
  640.4 11.3 bitcast_multiply_fusion
  651.7 15.4 bitcast_multiply_fusion.1
  667.1 10.3 fusion.50
  677.4 8.8 fusion.44
  686.2 10.6 add_bitcast_fusion
  696.8 12.4 copy.31
  709.2 26.4 %fusion.41 = f32[2,96,96,96]{2,3,1,0:T(8,128)} fusion(f32[2,96,96,96]{2,3,1,0:T(8,128)} %copy.31), kind=kOutput, calls=%fused_computation.50 | convolution fusion | flops 2038514688 | bytes 14155776 | tf_op jit(solution)/shard_map/kn,cxnz->cxkz/dot_general | solution.py:23
  735.7 23.6 %fusion.30 = f32[2,96,96,96]{2,3,1,0:T(8,128)} fusion(f32[2,96,96,96]{2,3,1,0:T(8,128)S(1)} %copy-done.3), kind=kOutput, calls=%fused_computation.39 | convolution fusion | flops 2038514688 | bytes 14155776 | tf_op jit(solution)/shard_map/kn,cxnz->cxkz/dot_general | solution.py:23
  759.4 10.6 subtract_bitcast_fusion
  769.9 12.5 copy.30
  782.5 24.6 %fusion.28 = f32[2,96,96,96]{2,3,1,0:T(8,128)S(1)} fusion(f32[2,96,96,96]{2,3,1,0:T(8,128)} %copy.30), kind=kOutput, calls=%fused_computation.37 | convolution fusion | flops 2038514688 | bytes 14155776 | tf_op jit(solution)/shard_map/kn,cxnz->cxkz/dot_general | solution.py:23
  807.1 23.4 %fusion.46 = f32[2,96,96,96]{2,3,1,0:T(8,128)} fusion(f32[2,96,96,96]{2,3,1,0:T(8,128)S(1)} %copy-done.4), kind=kOutput, calls=%fused_computation.55 | convolution fusion | flops 2038514688 | bytes 14155776 | tf_op jit(solution)/shard_map/kn,cxnz->cxkz/dot_general | solution.py:23
  830.5 10.2 fusion.7
  840.7 15.9 %multiply_convert_fusion = bf16[2,96,96,96]{3,2,1,0:T(8,128)(2,1)} fusion(f32[2,96,96,96]{3,2,1,0:T(8,128)} %fusion.7, f32[2,96,96,96]{2,3,1,0:T(8,128)} %fusion.46, f32[2,96,96,96]{2,3,1,0:T(8,128)} %fusion.30), kind=kOutput, calls=%fused_computation.16 | convolution fusion | flops 2045592576 | bytes 24772608 | tf_op jit(solution)/shard_map/kn,cxyn->cxyk/dot_general | solution.py:23
  856.6 7.8 all_to_all.29
  864.4 5.6 copy.24
  870.0 55.9 %all_to_all.35 = bf16[2,128,6912]{2,0,1:T(2,128)(2,1)} all-to-all(bf16[2,128,6912]{2,0,1:T(2,128)(2,1)S(1)} %copy.24), channel_id=1, replica_groups=mesh['grid'=64,'col'=2] {'grid','col'}, dimensions={1} | all-to-all | bytes 7077888 | tf_op jit(solution)/shard_map/all_to_all | solution.py:95
  926.0 8.3 all_to_all.32
  934.3 10.9 convolution_multiply_fusion.1
  945.1 637.2 %reduce-scatter.2.cloned.1.call-done = f32[8,256]{1,0:T(8,128)} async-done(((f32[1024,256]{1,0:T(8,128)}), f32[8,256]{1,0:T(8,128)}) %reduce-scatter.2.cloned.1.call-update) | async-done | bytes 8208 | tf_op jit(solution)/shard_map/reduce_scatter | solution.py:97
  (49 shorter events, 1.9 us)
Async XLA Ops:
  7.2 368.1 %copy-start = (bf16[1024,256]{1,0:T(8,128)(2,1)S(1)}, bf16[1024,256]{1,0:T(8,128)(2,1)}, u32[]{:S(2)}) copy-start(bf16[1024,256]{1,0:T(8,128)(2,1)} %param.7) | copy-start | bytes 1572868
  7.2 59.6 %all-reduce.3.cloned.1.call-start = ((), (), s32[]{:S(2)}) async-start(), calls=%async_computation.3 | async-start | bytes 2097152 | tf_op jit(solution)/shard_map/psum | solution.py:69
  396.1 90.2 %all-to-all-start = ((f32[128,2,6912]{2,1,0:T(2,128)}), f32[128,2,6912]{2,1,0:T(2,128)}, u32[]{:S(2)}, u32[]{:S(2)}) async-start(f32[128,2,6912]{2,1,0:T(2,128)} %all_to_all.26), calls=%async_computation | async-start | bytes 14155776 | tf_op jit(solution)/shard_map/all_to_all | solution.py:92
  401.9 1180.5 %reduce-scatter.2.cloned.1.call-start = ((), (), s32[]{:S(2)}) async-start(), calls=%async_computation.4 | async-start | bytes 1056768 | tf_op jit(solution)/shard_map/reduce_scatter | solution.py:97
  503.3 11.3 copy-start.6
  616.8 13.4 copy-start.5
  616.8 23.6 %slice-start = ((s8[4718592]{0:T(1024)(128)(4,1)}), s8[4194304]{0:T(1024)(128)(4,1)S(1)}, s32[]{:S(2)}) async-start(s8[4718592]{0:T(1024)(128)(4,1)} %bitcast.108), calls=%async_computation.5 | async-start | bytes 8388608
  630.2 10.2 slice-start.1
  651.7 25.7 %copy-start.2 = (f32[2,96,96,96]{1,3,2,0:T(8,128)}, f32[2,96,96,96]{1,3,2,0:T(8,128)S(1)}, u32[]{:S(2)}) copy-start(f32[2,96,96,96]{1,3,2,0:T(8,128)S(1)} %bitcast_multiply_fusion) | copy-start | bytes 21233668
  709.2 26.4 %copy-start.3 = (f32[2,96,96,96]{2,3,1,0:T(8,128)S(1)}, f32[2,96,96,96]{2,3,1,0:T(8,128)}, u32[]{:S(2)}) copy-start(f32[2,96,96,96]{2,3,1,0:T(8,128)} %copy.31) | copy-start | bytes 21233668
  709.2 50.1 %slice-start.2 = ((s8[9437184]{0:T(1024)(128)(4,1)}), s8[4194304]{0:T(1024)(128)(4,1)S(1)}, s32[]{:S(2)}) async-start(s8[9437184]{0:T(1024)(128)(4,1)} %bitcast.110), calls=%async_computation.7 | async-start | bytes 8388608
  709.2 50.1 %slice-start.3 = ((s8[9437184]{0:T(1024)(128)(4,1)}), s8[4194304]{0:T(1024)(128)(4,1)S(1)}, s32[]{:S(2)}) async-start(s8[9437184]{0:T(1024)(128)(4,1)} %bitcast.110), calls=%async_computation.8 | async-start | bytes 8388608
  709.2 50.1 %slice-start.5 = ((s8[9437184]{0:T(1024)(128)(4,1)}), s8[4194304]{0:T(1024)(128)(4,1)S(1)}, s32[]{:S(2)}) async-start(s8[9437184]{0:T(1024)(128)(4,1)} %bitcast.112), calls=%async_computation.10 | async-start | bytes 8388608
  709.2 50.1 %slice-start.6 = ((s8[9437184]{0:T(1024)(128)(4,1)}), s8[4194304]{0:T(1024)(128)(4,1)S(1)}, s32[]{:S(2)}) async-start(s8[9437184]{0:T(1024)(128)(4,1)} %bitcast.112), calls=%async_computation.11 | async-start | bytes 8388608
  735.7 23.7 %slice-start.4 = ((s8[9437184]{0:T(1024)(128)(4,1)}), s8[1048576]{0:T(1024)(128)(4,1)S(1)}, s32[]{:S(2)}) async-start(s8[9437184]{0:T(1024)(128)(4,1)} %bitcast.110), calls=%async_computation.9 | async-start | bytes 2097152
  735.7 23.7 %slice-start.7 = ((s8[9437184]{0:T(1024)(128)(4,1)}), s8[1048576]{0:T(1024)(128)(4,1)S(1)}, s32[]{:S(2)}) async-start(s8[9437184]{0:T(1024)(128)(4,1)} %bitcast.112), calls=%async_computation.12 | async-start | bytes 2097152
  782.5 24.6 %copy-start.4 = (f32[2,96,96,96]{2,3,1,0:T(8,128)S(1)}, f32[2,96,96,96]{2,3,1,0:T(8,128)}, u32[]{:S(2)}) copy-start(f32[2,96,96,96]{2,3,1,0:T(8,128)} %copy.30) | copy-start | bytes 21233668
  782.5 48.0 %slice-start.8 = ((s8[9437184]{0:T(1024)(128)(4,1)}), s8[4194304]{0:T(1024)(128)(4,1)S(1)}, s32[]{:S(2)}) async-start(s8[9437184]{0:T(1024)(128)(4,1)} %bitcast.114), calls=%async_computation.13 | async-start | bytes 8388608
  782.5 48.0 %slice-start.9 = ((s8[9437184]{0:T(1024)(128)(4,1)}), s8[4194304]{0:T(1024)(128)(4,1)S(1)}, s32[]{:S(2)}) async-start(s8[9437184]{0:T(1024)(128)(4,1)} %bitcast.114), calls=%async_computation.14 | async-start | bytes 8388608
  807.1 23.4 %slice-start.10 = ((s8[9437184]{0:T(1024)(128)(4,1)}), s8[1048576]{0:T(1024)(128)(4,1)S(1)}, s32[]{:S(2)}) async-start(s8[9437184]{0:T(1024)(128)(4,1)} %bitcast.114), calls=%async_computation.15 | async-start | bytes 2097152
  926.0 656.4 %copy-start.1 = (bf16[1024,256]{1,0:T(8,128)(2,1)S(1)}, bf16[1024,256]{1,0:T(8,128)(2,1)}, u32[]{:S(2)}) copy-start(bf16[1024,256]{1,0:T(8,128)(2,1)} %param.7) | copy-start | bytes 1572868
Sparse Core Ops, SparseCore 0:
  16.1 50.6 all-reduce.2
  945.3 637.0 reduce-scatter.1
